TPU v7x, 32 devices: a whole 2x2x4 slice. The times are simulated.
32 devices in a mesh: groups: 2 (over x), blk: 16 (over z, y, core).
Axes of the slice: x: 2, y: 2, z: 4, core: 2. Of those that a mesh axis runs over, the one named last changes fastest.
Arguments:
- records: bfloat16 [8192, 2048], P(('groups', 'blk')), parts along dimension 0, may hold values from -6 to 6
- dest: int32 [8192, 1], P(('groups', 'blk')), parts along dimension 0, may hold values from 0 to 15; in each aligned block of 256 rows (0 to 255, 256 to 511, ...) at most 32 rows name the same one
- slot: int32 [8192, 1], P(('groups', 'blk')), parts along dimension 0, may hold values from 0 to 255
- valid: int32 [8192, 1], P(('groups', 'blk')), parts along dimension 0, may hold values from 256 to 2048
- masks: int32 [2], replicated, may hold values from 1 to 15, as said below
Outputs:
- correlations: bfloat16 [2, 4096, 128, 128], P(None, ('groups', 'blk')), parts along dimension 1
There are 2 independent parts, one for each index of `groups`. A program takes and returns all parts, laid end to end along the dimension named above; an argument that names none is the same for every part. Nothing has to cross between parts.
Inputs may be any that keep to these rules, and one draw needn't show every extreme that they name: `dest`: in the rows of one device no block is named more than 32 times. `masks`: 2 distinct numbers; one of them is 15.
All inputs are finite; a program needn't handle non-finite values.
Results may differ from a plain program's by a relative error of at most 0.0085.
Values may be sent and summed in bfloat16 or wider, within the bound.
A program may use at most 128 MiB of HBM per device.

v0:
```python
import functools
import math

import jax
import jax.numpy as jnp
import numpy as np
from jax import lax
from jax.experimental import pallas as pl
from jax.experimental.pallas import tpu as pltpu
from jax.sharding import PartitionSpec as P

CH = 128
F = 256
LAGS = 128
W = 2
GROUP = 4
CHUNK = 256
AHEAD = 2
PIECES = 8
FLIGHT = 4
LAG = 3
GAP = 64.0
LEVELS = (
    ((96, 96, 96, 80, 64, 64, 48, 32), (64, 64, 64, 64, 48, 48, 32, 16)),
    ((112, 112, 96, 80, 64, 64, 48, 32), (64, 64, 64, 64, 48, 48, 32, 32)),
    ((112, 112, 112, 96, 80, 64, 48, 32), (64, 64, 64, 64, 48, 48, 32, 32)),
    ((128, 128, 112, 96, 80, 80, 64, 48), (64, 64, 64, 64, 64, 48, 48, 32)),
)
VMEM = pl.BlockSpec(memory_space=pltpu.VMEM)
SMEM = pl.BlockSpec(memory_space=pltpu.SMEM)
HBM = pl.BlockSpec(memory_space=pl.ANY)
MESH = pl.DeviceIdType.MESH


def forward_table(nfft, bins):
    sample = np.arange(nfft, dtype=np.int64)[:, None]
    freq = np.arange(1, bins + 1, dtype=np.int64)[None, :]
    angle = (sample * freq % nfft).astype(np.float32) * np.float32(2.0 * math.pi / nfft)
    return np.concatenate([np.cos(angle), -np.sin(angle)], axis=1).astype(jnp.bfloat16)


def lag_table(nfft, bins, lags):
    shift = (np.arange(lags, dtype=np.int64) - lags // 2) % nfft
    freq = np.arange(1, bins + 1, dtype=np.int64)[None, :]
    angle = (freq * shift[:, None] % nfft).astype(np.float32) * np.float32(2.0 * math.pi / nfft)
    return np.concatenate([np.cos(angle), -np.sin(angle)], axis=1).astype(jnp.bfloat16)


def met_at(me, distance, owners):
    other = me
    for k in range(owners.bit_length() - 1):
        if distance >> k & 1:
            other = other + (1 << k) * (1 - 2 * lax.rem(lax.div(me, 1 << k), 2))
    return other


def gathered_at(distance):
    bits = GROUP.bit_length() - 1
    return sum((distance >> k & 1) << (bits - 1 - k) for k in range(bits))


def split_at(planes, most):
    return planes == 4 and most >= 32


def kept_at(planes, most):
    return GROUP * planes * most * (3 if split_at(planes, most) else 4) // 4


def capacities(most, chunks):
    def scaled(level, bound, unit):
        rows = [-(-level[c * len(level) // chunks] * bound // (unit * 16)) * 16 for c in range(chunks)]
        return tuple(min(bound, max(16, r)) for r in rows)

    full = ((most,) * chunks, (most // 2,) * chunks)
    found = []
    for far, near in LEVELS:
        rows = (scaled(far, most, 128), scaled(near, most // 2, 64))
        if rows not in found and rows[0] != full[0]:
            found.append(rows)
    return found + [full]


def first_sends(planes, split):
    if not split:
        return [(d, 0, False) for d in range(planes - 1, -1, -1)]
    other = GROUP // 2
    return [(3, 0, False), (2, 0, False), (1, 0, True), (1, other, True), (0, other, True), (0, 0, True)]


def plan_kernel(
    records_ref, dest_ref, slot_ref, valid_ref,
    outgoing_ref, first_ref, goal_ref, level_ref,
    outbox, inbox, levels, send_sem, recv_sem, level_sems, first_sems, own_sem,
):
    chunks, planes, most, wide = outgoing_ref.shape
    owners = planes * GROUP
    held = records_ref.shape[0]
    me, part = lax.axis_index("blk"), lax.axis_index("groups")
    parts = levels.shape[0]
    shift = most.bit_length() - 1
    plane = lax.div(me, GROUP)

    barrier = pltpu.get_barrier_semaphore()
    for distance in range(1, owners):
        pl.semaphore_signal(
            barrier, inc=1, device_id={"blk": met_at(me, distance, owners)}, device_id_type=MESH
        )
    abroad = [
        (turn, distance, {"groups": lax.rem(part + turn, parts), "blk": met_at(me, distance, owners)})
        for turn in range(1, parts)
        for distance in range(owners)
    ]
    for _, _, other in abroad:
        pl.semaphore_signal(barrier, inc=1, device_id=other, device_id_type=MESH)

    dest, slot, valid = dest_ref[...], slot_ref[...], valid_ref[...]
    group, within = lax.div(dest, GROUP), lax.rem(dest, GROUP)
    key = valid * held + (held - 1 - lax.broadcasted_iota(jnp.int32, (1, held), 1))
    line = lax.broadcasted_iota(jnp.int32, (8, held), 0)
    split = split_at(planes, most)
    half = most // 2
    chip = lax.div(within, GROUP // 2)
    if split:
        near = (group >> 1) == lax.div(plane, 2)
    else:
        near = group < 0
    kind = group * 4 + jnp.where(near, 1 + chip, 0)
    columns = jnp.where(line == 0, kind, jnp.where(line == 1, key, valid)).astype(jnp.float32).T
    key, kind = key.astype(jnp.float32), kind.astype(jnp.float32)
    ahead = (columns[:, 1:2] > key) & (columns[:, 0:1] == kind)
    rank = jnp.sum(ahead.astype(jnp.float32), axis=0, keepdims=True).astype(jnp.int32)
    reach = lax.div(valid - 1, wide)
    level = jnp.zeros((1, held), jnp.float32)
    for far_rows, near_rows in capacities(most, chunks)[:-1]:
        limit = jnp.zeros((1, held), jnp.int32)
        for c in range(chunks):
            limit = jnp.where(reach == c, jnp.where(near, near_rows[c], far_rows[c]), limit)
        level = level + jnp.max((rank >= limit).astype(jnp.float32), axis=1, keepdims=True)
    levels[0, 0] = level[:, :128]
    rank = rank + jnp.where(near, chip * half, 0)

    lines = max(8, planes)
    named = lax.broadcasted_iota(jnp.int32, (lines, held), 0) == group
    ranked = (lax.broadcasted_iota(jnp.int32, (128, held), 0) == rank).astype(jnp.float32)
    ranked = ranked.astype(jnp.bfloat16)

    def spread(values):
        values = jnp.where(named, values, 0).astype(jnp.float32).astype(jnp.bfloat16)
        return lax.dot_general(
            values, ranked, (((1,), (1,)), ((), ())), preferred_element_type=jnp.float32
        )

    code = spread(within + 1) * 256.0 + spread(slot)
    for p in range(planes):
        outbox[p, 0:1, :] = code[p : p + 1]
        outbox[p, 1:2, :] = level[:, :128]

    spots = planes * most
    place = lax.broadcasted_iota(jnp.int32, (spots, held), 0) == group * most + rank
    place = place.astype(jnp.float32).astype(jnp.bfloat16)
    ends = columns[:, 2:3].astype(jnp.int32)

    def pack(c):
        window = lax.broadcasted_iota(jnp.int32, (held, wide), 1) + c * wide < ends
        window = window.astype(jnp.float32).astype(jnp.bfloat16)
        data = records_ref[:, c * wide : (c + 1) * wide] * window + (GAP - GAP * window)
        packed = jnp.dot(place, data, preferred_element_type=jnp.float32)
        outgoing_ref[c] = packed.astype(jnp.bfloat16).reshape(planes, most, wide)

    pack(0)
    pl.semaphore_wait(barrier, owners * parts - 1)
    copies = []
    for turn, distance, other in abroad:
        copies.append(
            pltpu.make_async_remote_copy(
                src_ref=levels.at[0, 0],
                dst_ref=levels.at[turn, distance],
                send_sem=level_sems.at[0, turn, distance],
                recv_sem=level_sems.at[1, turn, distance],
                device_id=other,
                device_id_type=MESH,
            )
        )
        copies[-1].start()
    for distance in range(owners - 1, 0, -1):
        other = met_at(me, distance, owners)
        copies.append(
            pltpu.make_async_remote_copy(
                src_ref=outbox.at[lax.div(other, GROUP)],
                dst_ref=inbox.at[gathered_at(distance % GROUP) * planes + plane],
                send_sem=send_sem.at[distance],
                recv_sem=recv_sem.at[distance],
                device_id={"blk": other},
                device_id_type=MESH,
            )
        )
        copies[-1].start()
    row = lax.rem(lax.div(me, GROUP // 2), 2)
    first = []
    for index, (d, turned, near) in enumerate(first_sends(planes, split)):
        other = met_at(me, GROUP * d + turned, owners)
        rows = pl.ds(0, most)
        if near:
            at = row if turned == 0 else 1 - row
            rows = pl.ds(pl.multiple_of(at * half, 16), half)
        source = outgoing_ref.at[0, lax.div(other, GROUP), rows]
        target = first_ref.at[1 if turned else 0, plane, rows]
        if d == 0 and turned == 0:
            first.append(pltpu.make_async_copy(source, target, own_sem))
        else:
            first.append(
                pltpu.make_async_remote_copy(
                    src_ref=source,
                    dst_ref=target,
                    send_sem=first_sems.at[0, index],
                    recv_sem=first_sems.at[1, index],
                    device_id={"blk": other},
                    device_id_type=MESH,
                )
            )
        first[-1].start()
    inbox[plane] = outbox[plane]

    for c in range(1, chunks):
        pack(c)

    kept = goal_ref.shape[1]
    at = lax.broadcasted_iota(jnp.int32, (1, kept), 1)
    source, spot = at >> shift, at & (most - 1)
    if split:
        near_base = lax.div(plane, 2) * 2
        far_base = 2 - near_base
        rest = at - GROUP * 2 * most
        source = jnp.where(
            rest < 0,
            (at >> (shift + 1)) * planes + far_base + ((at >> shift) & 1),
            (rest >> shift) * planes + near_base + ((rest >> (shift - 1)) & 1),
        )
        spot = jnp.where(rest < 0, spot, row * half + (rest & (half - 1)))
    sown = lax.broadcasted_iota(jnp.int32, (128, kept), 0) == spot
    sown = sown.astype(jnp.float32).astype(jnp.bfloat16)
    for copy in copies:
        copy.wait()
    code = inbox[:, 0, :]
    level = jnp.max(inbox[:, 1, :], axis=0, keepdims=True)
    for turn, distance, _ in abroad:
        level = jnp.maximum(level, levels[turn, distance])
    level_ref[0] = jnp.max(level).astype(jnp.int32)
    owner = (code * (1.0 / 256.0)).astype(jnp.int32).astype(jnp.float32)
    slots = code - owner * 256.0
    mine = lax.broadcasted_iota(jnp.int32, (owners, kept), 0) == source

    def line_up(values):
        values = jnp.dot(values.astype(jnp.bfloat16), sown, preferred_element_type=jnp.float32)
        return jnp.sum(jnp.where(mine, values, 0.0), axis=0, keepdims=True).astype(jnp.int32)

    slots = line_up(slots)
    goal = (slots & (W - 1)) * CH + (slots >> (W.bit_length() - 1))
    goal_ref[...] = jnp.where(line_up(owner) == lax.rem(me, GROUP) + 1, goal, -1)
    for copy in first:
        copy.wait()


def deliver_kernel(
    caps, outgoing_ref, first_ref, goal_ref, masks_ref, table_hbm,
    own_ref, met_ref,
    arrived, select, table, spectrum, energy, tile, leaving, landing,
    plane_send, plane_recv, gather_send, gather_recv, own_sem, table_sem,
    far_send, far_recv, hop_send, hop_recv,
):
    chunks, _, planes, most, wide = arrived.shape
    owners = planes * GROUP
    nfft = chunks * wide
    kept = goal_ref.shape[1]
    me = lax.axis_index("blk")
    plane = lax.div(me, GROUP)
    last = owners - 1
    bits = list(range(owners.bit_length() - 3, -1, -1))
    split = split_at(planes, most)
    half = most // 2
    row = lax.rem(lax.div(me, GROUP // 2), 2)
    near_base = lax.div(plane, 2) * 2
    far_planes = pl.ds(2 - near_base, 2) if split else pl.ds(0, planes)
    near_planes = pl.ds(near_base, 2)

    barrier = pltpu.get_barrier_semaphore()
    sends = first_sends(planes, split)
    peers = {GROUP * d + turned for d, turned, _ in sends} - {0}
    peers |= {GROUP // 2, 1} | {1 << k for k in bits} | {last}
    for distance in sorted(peers):
        pl.semaphore_signal(
            barrier, inc=1, device_id={"blk": met_at(me, distance, owners)}, device_id_type=MESH
        )
    fetch = pltpu.make_async_copy(table_hbm, table, table_sem)
    fetch.start()
    pl.semaphore_wait(barrier, len(peers))

    def send(distance, source, target, send_sem, recv_sem):
        copy = pltpu.make_async_remote_copy(
            src_ref=source,
            dst_ref=target,
            send_sem=send_sem,
            recv_sem=recv_sem,
            device_id={"blk": met_at(me, distance, owners)},
            device_id_type=MESH,
        )
        copy.start()
        return copy

    sent, local, gathers = {}, {}, {}

    def some(at, count):
        return pl.ds(pl.multiple_of(at * half, 16), count)

    def begin(c):
        for index, (d, turned, near) in enumerate(sends):
            other = lax.div(met_at(me, GROUP * d + turned, owners), GROUP)
            rows = pl.ds(0, caps[0][c])
            if near:
                rows = some(row if turned == 0 else 1 - row, caps[1][c])
            source = outgoing_ref.at[c, other, rows]
            target = arrived.at[c, 1 if turned else 0, plane, rows]
            if d == 0 and turned == 0:
                sent[c, index] = pltpu.make_async_copy(source, target, own_sem.at[c])
                sent[c, index].start()
            else:
                sent[c, index] = send(
                    GROUP * d + turned, source, target, plane_send.at[c, index], plane_recv.at[c, index]
                )

    def region(c, near):
        if near:
            return near_planes, some(row, caps[1][c])
        return far_planes, pl.ds(0, caps[0][c])

    def forward(c, which, early=False):
        planes_at, rows = region(c, which in (2, 4))
        held_at = 1 if which in (3, 4) else 0
        source = first_ref if early else arrived.at[c]
        gathers[c, which] = send(
            GROUP // 2 if which == 0 else 1,
            source.at[held_at, planes_at, rows],
            arrived.at[c, held_at + (1 if which == 0 else 2), planes_at, rows],
            gather_send.at[c, which],
            gather_recv.at[c, which],
        )

    def forward_first():
        forward(0, 0, True)
        forward(0, 1, True)
        for index, (held_at, near) in enumerate([(0, False), (0, True), (1, True)]):
            if near and not split:
                continue
            planes_at, rows = region(0, near)
            local[index] = pltpu.make_async_copy(
                first_ref.at[held_at, planes_at, rows],
                arrived.at[0, held_at, planes_at, rows],
                own_sem.at[chunks + index],
            )
            local[index].start()
            if near:
                forward(0, 2 * held_at + 2, True)

    ahead = min(AHEAD, chunks - 1)
    forward_first()
    for c in range(1, 1 + ahead):
        begin(c)
    def blank(c, planes_at, rows):
        rest = arrived.at[c, :, planes_at, rows, :]
        rest[...] = jnp.full(rest.shape, GAP, jnp.bfloat16)

    for c in range(chunks):
        if caps[0][c] < most:
            blank(c, far_planes, pl.ds(caps[0][c], most - caps[0][c]))
        if split:
            if caps[1][c] < half:
                start = pl.multiple_of(row * half + caps[1][c], 16)
                blank(c, near_planes, pl.ds(start, half - caps[1][c]))
    goal = goal_ref[...]
    width = min(512, kept)
    for base in range(0, kept, width):
        chosen = lax.broadcasted_iota(jnp.int32, (CH * W, width), 0) == goal[:, base : base + width]
        select[:, base : base + width] = chosen.astype(jnp.float32).astype(jnp.bfloat16)

    def compute(c):
        if split:
            data = jnp.concatenate(
                [
                    arrived[c, :, far_planes].reshape(2 * GROUP * most, wide),
                    arrived[c, :, near_planes, some(row, half)].reshape(2 * GROUP * half, wide),
                ],
                axis=0,
            )
        else:
            data = arrived[c].reshape(kept, wide)
        window = jnp.minimum(jnp.maximum(GAP / 2 - data, 0.0), 1.0)
        total = jnp.dot(select[...], data * window, preferred_element_type=jnp.float32)
        count = jnp.dot(select[...], window, preferred_element_type=jnp.float32)
        trace = total / jnp.maximum(count, 1.0)
        squares = trace * trace
        squares = sum(squares[:, k : k + 128] for k in range(0, wide, 128))
        part = jnp.dot(
            trace.astype(jnp.bfloat16),
            table[c * wide : (c + 1) * wide, :],
            preferred_element_type=jnp.float32,
        )
        if c == 0:
            energy[...], spectrum[...] = squares, part
        else:
            energy[...] += squares
            spectrum[...] += part

    for turn in range(1, chunks + 2):
        for stage in range(3):
            c = turn - stage
            if not 0 <= c < chunks:
                continue
            if stage == 0:
                if c + ahead < chunks:
                    begin(c + ahead)
                for index, (_, _, near) in enumerate(sends):
                    if not near:
                        (sent[c, index].wait_recv if sends[index][:2] != (0, 0) else sent[c, index].wait)()
                forward(c, 0)
                forward(c, 1)
                for index, (d, turned, near) in enumerate(sends):
                    if near:
                        (sent[c, index].wait_recv if d + turned else sent[c, index].wait)()
                if split:
                    forward(c, 2)
                    forward(c, 4)
            elif stage == 1:
                gathers[c, 0].wait_recv()
                forward(c, 3)
            else:
                for which in range(1, 5):
                    if (c, which) in gathers:
                        gathers[c, which].wait_recv()
                if c == 0:
                    fetch.wait()
                    for copy in local.values():
                        copy.wait()
                compute(c)

    second = masks_ref[0] ^ masks_ref[1] ^ last
    use_far = lax.div(second, 1 << (len(bits)))
    path = second + use_far * (last - 2 * second)
    size = CH // PIECES

    def choose(flag, yes, no):
        flag = jnp.full(yes.shape, flag.astype(jnp.float32), jnp.float32).astype(jnp.bfloat16)
        return yes * flag + no * (1 - flag)

    factor = lax.rsqrt(jnp.sum(energy[...], axis=1, keepdims=True) * (1.0 / nfft) + 1e-06)
    far = []

    def far_copy(q):
        rows = pl.ds(q * size, size)
        far.append(send(last, tile.at[rows], met_ref.at[rows], far_send.at[q], far_recv.at[q]))

    for q in range(PIECES):
        rows = slice(q * size, (q + 1) * size)
        for w in range(W):
            at = slice(w * CH + q * size, w * CH + (q + 1) * size)
            parts = spectrum[at, :] * factor[at]
            real_part, imag_part = parts[:, :F], parts[:, F:]
            amplitude = lax.rsqrt(
                jnp.maximum(real_part * real_part + imag_part * imag_part, nfft / 4.0)
            )
            real_part = (real_part * amplitude).astype(jnp.bfloat16)
            imag_part = (imag_part * amplitude).astype(jnp.bfloat16)
            base = 2 * F * w
            tile[rows, base : base + F] = real_part
            tile[rows, base + F : base + 2 * F] = imag_part
            own_ref[rows, base : base + F] = real_part.astype(jnp.float32)
            own_ref[rows, base + F : base + 2 * F] = imag_part.astype(jnp.float32)
        if q < FLIGHT:
            far_copy(q)

    hops = {}
    for turn in range(PIECES + LAG * len(bits)):
        for stage in range(len(bits) + 1):
            q = turn - LAG * stage
            if not 0 <= q < PIECES:
                continue
            rows = slice(q * size, (q + 1) * size)
            if stage == 0:
                far[q].wait_recv()
                if q + FLIGHT < PIECES:
                    far_copy(q + FLIGHT)
                value = choose(use_far, met_ref[rows], tile[rows])
            else:
                hops[stage - 1, q].wait_recv()
                taken = lax.rem(lax.div(path, 1 << bits[stage - 1]), 2)
                value = choose(taken, landing[stage - 1, rows], leaving[stage - 1, rows])
            if stage == len(bits):
                met_ref[CH + q * size : CH + (q + 1) * size] = value
            else:
                leaving[stage, rows] = value
                spot = pl.ds(q * size, size)
                hops[stage, q] = send(
                    1 << bits[stage],
                    leaving.at[stage, spot],
                    landing.at[stage, spot],
                    hop_send.at[stage, q],
                    hop_recv.at[stage, q],
                )
    abroad = [copy for (_, index), copy in sent.items() if sends[index][:2] != (0, 0)]
    for copy in abroad + list(gathers.values()) + far + list(hops.values()):
        copy.wait_send()


def correlate_kernel(masks_ref, own_ref, other_ref, table_ref, out_ref, turned, *, last):
    scale = 1.0 / math.sqrt(W * F)
    cosine, sine = table_ref[:, :F], table_ref[:, F:]
    far_round = (masks_ref[0] != last).astype(jnp.int32)
    slots, step = turned.shape[0], own_ref.shape[1]

    for index in range(step // 2):
        at = index % slots
        for half in range(2):
            mine = own_ref[0, index * 2 + half : index * 2 + half + 1, :].astype(jnp.bfloat16)
            rows = slice(half * LAGS, (half + 1) * LAGS)
            for w in range(W):
                base = 2 * F * w
                ur, ui = mine[:, base : base + F], mine[:, base + F : base + 2 * F]
                turned[at, rows, base : base + F] = cosine * ur + sine * ui
                turned[at, rows, base + F : base + 2 * F] = cosine * ui - sine * ur
        product = lax.dot_general(
            other_ref[...],
            turned[at],
            (((1,), (1,)), ((), ())),
            preferred_element_type=jnp.float32,
        )
        product = (product * scale).astype(jnp.bfloat16)
        for half in range(2):
            lags = slice(half * LAGS, (half + 1) * LAGS)
            out_ref[far_round, index * 2 + half] = product[:CH, lags]
            out_ref[1 - far_round, index * 2 + half] = product[CH:, lags]


def local(records, dest, slot, valid, masks):
    owners, parts = lax.axis_size("blk"), lax.axis_size("groups")
    held, nfft = records.shape
    rounds = masks.shape[0]
    planes, chunks = owners // GROUP, nfft // CHUNK
    most = max(16, GROUP * 2 * held // owners)
    width = 2 * F * W
    limit = 56 * 2**20
    outgoing, first, goal, level = pl.pallas_call(
        plan_kernel,
        out_shape=[
            jax.ShapeDtypeStruct((chunks, planes, most, CHUNK), jnp.bfloat16),
            jax.ShapeDtypeStruct((2, planes, most, CHUNK), jnp.bfloat16),
            jax.ShapeDtypeStruct((1, kept_at(planes, most)), jnp.int32),
            jax.ShapeDtypeStruct((1,), jnp.int32),
        ],
        in_specs=[VMEM] * 4,
        out_specs=[VMEM, VMEM, VMEM, SMEM],
        scratch_shapes=[
            pltpu.VMEM((planes, 2, 128), jnp.float32),
            pltpu.VMEM((owners, 2, 128), jnp.float32),
            pltpu.VMEM((parts, owners, 1, 128), jnp.float32),
            pltpu.SemaphoreType.DMA((owners,)),
            pltpu.SemaphoreType.DMA((owners,)),
            pltpu.SemaphoreType.DMA((2, parts, owners)),
            pltpu.SemaphoreType.DMA((2, planes + 2)),
            pltpu.SemaphoreType.DMA,
        ],
        compiler_params=pltpu.CompilerParams(
            vmem_limit_bytes=limit, collective_id=0, has_side_effects=True
        ),
        name="plan",
    )(records, dest.reshape(1, held), slot.reshape(1, held), valid.reshape(1, held))

    last = owners - 1
    hops = owners.bit_length() - 2

    def deliver(number, caps):
        def call(outgoing, first, goal, masks, table):
            return pl.pallas_call(
                functools.partial(deliver_kernel, caps),
                out_shape=[
                    jax.ShapeDtypeStruct((CH, width), jnp.float32),
                    jax.ShapeDtypeStruct((rounds * CH, width), jnp.bfloat16),
                ],
                in_specs=[HBM, HBM, VMEM, SMEM, HBM],
                out_specs=[VMEM] * 2,
                scratch_shapes=[
                    pltpu.VMEM((chunks, GROUP, planes, most, CHUNK), jnp.bfloat16),
                    pltpu.VMEM((CH * W, kept_at(planes, most)), jnp.bfloat16),
                    pltpu.VMEM((nfft, 2 * F), jnp.bfloat16),
                    pltpu.VMEM((CH * W, 2 * F), jnp.float32),
                    pltpu.VMEM((CH * W, 128), jnp.float32),
                    pltpu.VMEM((CH, width), jnp.bfloat16),
                    pltpu.VMEM((hops, CH, width), jnp.bfloat16),
                    pltpu.VMEM((hops, CH, width), jnp.bfloat16),
                    pltpu.SemaphoreType.DMA((chunks, planes + 2)),
                    pltpu.SemaphoreType.DMA((chunks, planes + 2)),
                    pltpu.SemaphoreType.DMA((chunks, 5)),
                    pltpu.SemaphoreType.DMA((chunks, 5)),
                    pltpu.SemaphoreType.DMA((chunks + 3,)),
                    pltpu.SemaphoreType.DMA,
                    pltpu.SemaphoreType.DMA((PIECES,)),
                    pltpu.SemaphoreType.DMA((PIECES,)),
                    pltpu.SemaphoreType.DMA((hops, PIECES)),
                    pltpu.SemaphoreType.DMA((hops, PIECES)),
                ],
                compiler_params=pltpu.CompilerParams(
                    vmem_limit_bytes=limit, collective_id=number, has_side_effects=True
                ),
                name=f"deliver{number}",
            )(outgoing, first, goal, masks, table)

        return call

    sizes = capacities(most, chunks)
    calls = [deliver(number + 1, caps) for number, caps in enumerate(sizes)]
    own, other = lax.switch(
        level[0], calls, outgoing, first, goal, masks, jnp.asarray(forward_table(nfft, F))
    )
    step = 32
    return pl.pallas_call(
        functools.partial(correlate_kernel, last=last),
        grid=(CH // step,),
        out_shape=jax.ShapeDtypeStruct((rounds, CH, CH, LAGS), jnp.bfloat16),
        in_specs=[
            SMEM,
            pl.BlockSpec((1, step, width), lambda i: (i, 0, 0)),
            pl.BlockSpec((rounds * CH, width), lambda i: (0, 0)),
            pl.BlockSpec((LAGS, 2 * F), lambda i: (0, 0)),
        ],
        out_specs=pl.BlockSpec((rounds, step, CH, LAGS), lambda i: (0, i, 0, 0)),
        scratch_shapes=[pltpu.VMEM((4, 2 * LAGS, width), jnp.bfloat16)],
        compiler_params=pltpu.CompilerParams(vmem_limit_bytes=limit),
        name="correlate",
    )(
        masks,
        own.reshape(CH // step, step, width),
        other,
        jnp.asarray(lag_table(nfft, F, LAGS)),
    )


def solution(mesh):
    return jax.shard_map(
        local,
        mesh=mesh,
        in_specs=(
            P(("groups", "blk"), None),
            P(("groups", "blk"), None),
            P(("groups", "blk"), None),
            P(("groups", "blk"), None),
            P(),
        ),
        out_specs=P(None, ("groups", "blk"), None, None),
        check_vma=False,
    )
```

profile of v0, /device:TPU:1, one launch (start us, length us, event | category | flops | bytes accessed | tf_op | source)
XLA Modules:
  0.0 85.1 jit_solution(13290709592604913669)
XLA Ops:
  0.0 17.0 %plan.1 = (bf16[8,4,128,256]{3,2,1,0:T(8,128)(2,1)S(1)}, bf16[2,4,128,256]{3,2,1,0:T(8,128)(2,1)S(1)}, s32[1,1536]{1,0:T(1,128)S(1)}, s32[1]{0:T(128)}) custom-call(bf16[256,2048]{1,0:T(8,128)(2,1)} %records_ref.1, s32[1,256]{1,0:T(1,128)} %bitcast.14, s32[1,256]{1,0:T(1,128)} %bitcast.15, s32[1,256]{1,0:T(1,128)} %bitcast.16), custom_call_target="tpu_custom_call" | custom-call | tf_op jit(solution)/shard_map/plan/pallas_call | solution.py:551
  17.6 55.6 %conditional.1 = (bf16[256,1024]{1,0:T(8,128)(2,1)S(1)}, f32[4,32,1024]{2,1,0:T(8,128)S(1)}) conditional(s32[]{:T(128)} %bitcast.8, (bf16[8,4,128,256]{3,2,1,0:T(8,128)(2,1)S(1)}, bf16[2,4,128,256]{3,2,1,0:T(8,128)(2,1)S(1)}, s32[1,1536]{1,0:T(1,128)S(1)}, s32[2]{0:T(128)}, bf16[2048,512]{1,0:T(8,128)(2,1)}) %tuple.30, ...), branch_computations={%region_0.0_spmd, %region_1.0_spmd, %region_2.0_spmd, %region_3.0_... | conditional | bytes 16 | solution.py:620
  17.6 54.8 %deliver1.1 = (f32[128,1024]{1,0:T(8,128)S(1)}, bf16[256,1024]{1,0:T(8,128)(2,1)S(1)}) custom-call(bf16[8,4,128,256]{3,2,1,0:T(8,128)(2,1)S(1)} %get-tuple-element.66.outgoing_ref, bf16[2,4,128,256]{3,2,1,0:T(8,128)(2,1)S(1)} %get-tuple-element.67.first_ref, s32[1,1536]{1,0:T(1,128)S(1)} %get-tuple-element.68.goal_ref, s32[2]{0:T(128)} %get-tuple-element.69.masks_ref, ...), custom_call_target="tpu_custom_call" | custom-call | tf_op jit(solution)/shard_map/cond/branch_0_fun/deliver1/pallas_call | solution.py:582
  73.2 12.0 %correlate.1 = bf16[2,128,128,128]{3,2,1,0:T(8,128)(2,1)} custom-call(s32[2]{0:T(128)} %masks_ref.1, f32[4,32,1024]{2,1,0:T(8,128)S(1)} %get-tuple-element.111.own_ref, bf16[256,1024]{1,0:T(8,128)(2,1)S(1)} %get-tuple-element.112.other_ref, bf16[128,512]{1,0:T(8,128)(2,1)} %constant.11.clone.table_ref), custom_call_target="tpu_custom_call" | custom-call | tf_op jit(solution)/shard_map/correlate/pallas_call | solution.py:624
where the time goes:
time: 85.3 us; the launch traced here: 85.1 us
  Pallas kernels  83.8 us (98%)
    pallas_call x1, Pallas kernels, call(): pl.pallas_call(functools.partial(deliver_kernel, caps), out_shape=[jax.Sh...  54.8 us
    pallas_call x1, Pallas kernels, local(): pl.pallas_call(plan_kernel, out_shape=[jax.ShapeDtypeStruct((chunks, plan...  17 us
    pallas_call x1, Pallas kernels, local(): pl.pallas_call(functools.partial(correlate_kernel, last=last), grid=(CH /...  12 us

commit v1 on v0

--- a/solution.py
+++ b/solution.py
@@ -363,9 +363,9 @@
                 forward(0, 2 * held_at + 2, True)
 
     ahead = min(AHEAD, chunks - 1)
-    forward_first()
     for c in range(1, 1 + ahead):
         begin(c)
+    forward_first()
     def blank(c, planes_at, rows):
         rest = arrived.at[c, :, planes_at, rows, :]
         rest[...] = jnp.full(rest.shape, GAP, jnp.bfloat16)

time: 85.3 us -> 85.1 us (level)
  no operation moved by 1% of the time
where the time goes in v1:
time: 85.1 us; the launch traced here: 85 us
  Pallas kernels  83.7 us (98%)
    pallas_call x1, Pallas kernels, call(): pl.pallas_call(functools.partial(deliver_kernel, caps), out_shape=[jax.Sh...  54.7 us
    pallas_call x1, Pallas kernels, local(): pl.pallas_call(plan_kernel, out_shape=[jax.ShapeDtypeStruct((chunks, plan...  17 us
    pallas_call x1, Pallas kernels, local(): pl.pallas_call(functools.partial(correlate_kernel, last=last), grid=(CH /...  12 us

profile of v1, /device:TPU:1, one launch (start us, length us, event | category | flops | bytes accessed | tf_op | source)
XLA Modules:
  0.0 85.0 jit_solution(2616651542384521329)
XLA Ops:
  0.0 17.0 %plan.1 = (bf16[8,4,128,256]{3,2,1,0:T(8,128)(2,1)S(1)}, bf16[2,4,128,256]{3,2,1,0:T(8,128)(2,1)S(1)}, s32[1,1536]{1,0:T(1,128)S(1)}, s32[1]{0:T(128)}) custom-call(bf16[256,2048]{1,0:T(8,128)(2,1)} %records_ref.1, s32[1,256]{1,0:T(1,128)} %bitcast.14, s32[1,256]{1,0:T(1,128)} %bitcast.15, s32[1,256]{1,0:T(1,128)} %bitcast.16), custom_call_target="tpu_custom_call" | custom-call | tf_op jit(solution)/shard_map/plan/pallas_call | solution.py:551
  17.6 55.4 %conditional.1 = (bf16[256,1024]{1,0:T(8,128)(2,1)S(1)}, f32[4,32,1024]{2,1,0:T(8,128)S(1)}) conditional(s32[]{:T(128)} %bitcast.8, (bf16[8,4,128,256]{3,2,1,0:T(8,128)(2,1)S(1)}, bf16[2,4,128,256]{3,2,1,0:T(8,128)(2,1)S(1)}, s32[1,1536]{1,0:T(1,128)S(1)}, s32[2]{0:T(128)}, bf16[2048,512]{1,0:T(8,128)(2,1)}) %tuple.30, ...), branch_computations={%region_0.0_spmd, %region_1.0_spmd, %region_2.0_spmd, %region_3.0_... | conditional | bytes 16 | solution.py:620
  17.6 54.7 %deliver1.1 = (f32[128,1024]{1,0:T(8,128)S(1)}, bf16[256,1024]{1,0:T(8,128)(2,1)S(1)}) custom-call(bf16[8,4,128,256]{3,2,1,0:T(8,128)(2,1)S(1)} %get-tuple-element.66.outgoing_ref, bf16[2,4,128,256]{3,2,1,0:T(8,128)(2,1)S(1)} %get-tuple-element.67.first_ref, s32[1,1536]{1,0:T(1,128)S(1)} %get-tuple-element.68.goal_ref, s32[2]{0:T(128)} %get-tuple-element.69.masks_ref, ...), custom_call_target="tpu_custom_call" | custom-call | tf_op jit(solution)/shard_map/cond/branch_0_fun/deliver1/pallas_call | solution.py:582
  73.0 12.0 %correlate.1 = bf16[2,128,128,128]{3,2,1,0:T(8,128)(2,1)} custom-call(s32[2]{0:T(128)} %masks_ref.1, f32[4,32,1024]{2,1,0:T(8,128)S(1)} %get-tuple-element.111.own_ref, bf16[256,1024]{1,0:T(8,128)(2,1)S(1)} %get-tuple-element.112.other_ref, bf16[128,512]{1,0:T(8,128)(2,1)} %constant.11.clone.table_ref), custom_call_target="tpu_custom_call" | custom-call | tf_op jit(solution)/shard_map/correlate/pallas_call | solution.py:624
